TPU v7x, 32 devices: a whole 2x2x4 slice. The times are simulated.
32 devices in a mesh: dp: 8 (over y, x, core), strip: 4 (over z).
Axes of the slice: x: 2, y: 2, z: 4, core: 2. Of those that a mesh axis runs over, the one named last changes fastest.
Arguments:
- latents: bfloat16 [8, 4, 320, 128], P('dp', 'strip'), may hold values from -6 to 6
- cotangent: bfloat16 [8, 4, 320, 128], P('dp', 'strip'), may hold values from -6 to 6
- weight: bfloat16 [320, 2880], P('strip'), may hold values from -0.109375 to 0.109375
- master: float32 [336, 2880], P('dp'), may hold values from -0.21875 to 0.21875
- first_moment: float32 [336, 2880], P('dp'), may hold values from -6 to 6
- second_moment: float32 [336, 2880], P('dp'), may hold values from 0.005 to 0.05
- owner_list: int32 [320], replicated, may hold values from 0 to 7, as said below
Outputs:
- output: bfloat16 [8, 4, 320, 128], P('dp', 'strip')
- grad_input: bfloat16 [8, 4, 320, 128], P('dp', 'strip')
- new_weight: bfloat16 [320, 2880], P('strip')
- new_master: float32 [336, 2880], P('dp')
- new_first: float32 [336, 2880], P('dp')
- new_second: float32 [336, 2880], P('dp')
Inputs may be any that keep to these rules, and one draw needn't show every extreme that they name: `owner_list`: each of the 8 ranks owns at least one and at most 42 buckets, and some rank owns exactly 42.
All inputs are finite; a program needn't handle non-finite values.
Results may differ from a plain program's by a relative error of at most 0.0033.
Values may be sent and summed in bfloat16 or wider, within the bound.
A program may use at most 64 MiB of HBM per device.

v0:
```python
import jax
import jax.numpy as jnp
from jax import lax
from jax.sharding import PartitionSpec as P

beta_first = 0.9
beta_second = 0.999
learn_rate = 0.01
epsilon = 1e-08
bias_first = 1.0 - 0.9**10
bias_second = 1.0 - 0.999**10


def extended(cells, sides, width):
    for axis, dim in sides:
        count = lax.axis_size(axis)
        ends = count - 1
        head = lax.slice_in_dim(cells, 0, width, axis=dim)
        tail = lax.slice_in_dim(cells, cells.shape[dim] - width, cells.shape[dim], axis=dim)
        cells = jnp.concatenate(
            [
                lax.ppermute(tail, axis, [(i, (i + 1) % count) for i in range(ends)]),
                cells,
                lax.ppermute(head, axis, [((i + 1) % count, i) for i in range(ends)]),
            ],
            axis=dim,
        )
    return cells


def patches(padded, direction):
    widened = jnp.pad(padded, ((0, 0), (0, 0), (1, 1)))
    height = padded.shape[0] - 2
    across = padded.shape[2]
    pieces = []
    for row_step in (-1, 0, 1):
        for col_step in (-1, 0, 1):
            row_start = 1 + direction * row_step
            col_start = 1 + direction * col_step
            pieces.append(
                widened[row_start : row_start + height, :, col_start : col_start + across]
            )
    return jnp.concatenate(pieces, axis=1)


def flipped(weight):
    channels = weight.shape[0]
    return weight.reshape(channels, 9, channels).transpose(2, 1, 0).reshape(channels, 9 * channels)


def slot_tables(owner_list, capacity):
    count = owner_list.shape[0]
    same_owner = owner_list[:, None] == owner_list[None, :]
    earlier = (
        jnp.arange(count, dtype=jnp.int32)[None, :] < jnp.arange(count, dtype=jnp.int32)[:, None]
    )
    within = jnp.sum((same_owner & earlier).astype(jnp.int32), axis=1)
    return owner_list * capacity + within


def adam_update(grads, master, first_moment, second_moment, filled):
    first_new = beta_first * first_moment + (1.0 - beta_first) * grads
    second_new = beta_second * second_moment + (1.0 - beta_second) * grads * grads
    update = learn_rate * (first_new / bias_first) / (jnp.sqrt(second_new / bias_second) + epsilon)
    keep = filled[:, None]
    return (
        jnp.where(keep, master - update, master),
        jnp.where(keep, first_new, first_moment),
        jnp.where(keep, second_new, second_moment),
    )


def local(latents, cotangent, weight, master, first_moment, second_moment, owner_list):
    full_weight = lax.all_gather(weight, "strip", axis=0, tiled=True)
    channels = full_weight.shape[0]
    pixels = latents[0]
    upstream = cotangent[0]
    pixels_float = pixels.astype(jnp.float32)
    active = jax.nn.silu(pixels_float).astype(jnp.bfloat16)
    active_rim = extended(active, (("strip", 0),), 1)
    forward_cols = patches(active_rim, 1)
    convolved = jnp.einsum(
        "ok,hkw->how", full_weight, forward_cols, preferred_element_type=jnp.float32
    )
    output = (pixels_float + convolved).astype(jnp.bfloat16)
    upstream_rim = extended(upstream, (("strip", 0),), 1)
    backward_cols = patches(upstream_rim, -1)
    spread = jnp.einsum(
        "ck,hkw->hcw", flipped(full_weight), backward_cols, preferred_element_type=jnp.float32
    )
    sigmoid_val = jax.nn.sigmoid(pixels_float)
    derivative = sigmoid_val * (1.0 + pixels_float * (1.0 - sigmoid_val))
    grad_input = (upstream.astype(jnp.float32) + spread * derivative).astype(jnp.bfloat16)
    partial_grad = jnp.einsum(
        "how,hkw->ok", upstream, forward_cols, preferred_element_type=jnp.float32
    )
    capacity = master.shape[0]
    owners = lax.axis_size("dp")
    owner_rank = lax.axis_index("dp")
    slot_ids = slot_tables(owner_list, capacity)
    matches = slot_ids[None, :] == jnp.arange(owners * capacity, dtype=jnp.int32)[:, None]
    bucket = jnp.sum(jnp.where(matches, jnp.arange(channels, dtype=jnp.int32)[None, :], 0), axis=1)
    filled = jnp.any(matches, axis=1)
    source_row = jnp.where(filled, bucket, channels)
    my_filled = lax.dynamic_slice_in_dim(filled, owner_rank * capacity, capacity)
    outgoing = jnp.take(partial_grad, source_row, axis=0, mode="fill", fill_value=0.0).reshape(
        owners, capacity, 9 * channels
    )
    incoming = lax.all_to_all(
        outgoing.astype(jnp.bfloat16), "dp", split_axis=0, concat_axis=0, tiled=True
    ).astype(outgoing.dtype)
    owned_grad = lax.psum(jnp.sum(incoming, axis=0).astype(jnp.bfloat16), "strip").astype(
        jnp.float32
    )
    pixel_count = (
        latents.shape[0] * owners * pixels.shape[0] * lax.axis_size("strip") * pixels.shape[2]
    )
    gradient = owned_grad / jnp.sqrt(jnp.float32(pixel_count))
    new_master, new_first, new_second = adam_update(
        gradient, master, first_moment, second_moment, my_filled
    )
    published = lax.all_gather(new_master.astype(jnp.bfloat16), "dp", axis=0, tiled=True)
    quarter = weight.shape[0]
    wanted = lax.dynamic_slice_in_dim(slot_ids, lax.axis_index("strip") * quarter, quarter)
    new_weight = published[wanted]
    return (output[None], grad_input[None], new_weight, new_master, new_first, new_second)


def solution(mesh):
    in_specs = (
        P("dp", "strip", None, None),
        P("dp", "strip", None, None),
        P("strip", None),
        P("dp", None),
        P("dp", None),
        P("dp", None),
        P(),
    )
    out_specs = (
        P("dp", "strip", None, None),
        P("dp", "strip", None, None),
        P("strip", None),
        P("dp", None),
        P("dp", None),
        P("dp", None),
    )
    return jax.shard_map(local, mesh=mesh, in_specs=in_specs, out_specs=out_specs, check_vma=False)
```

profile of v0, /device:TPU:0, one launch (start us, length us, event | category | flops | bytes accessed | tf_op | source)
XLA Modules:
  0.0 179.4 jit_solution(16090819397712765785)
XLA Ops:
  7.2 0.9 fusion.22
  8.2 1.3 collective-permute-start.1
  9.5 5.6 %collective-permute-start = (bf16[1,320,128]{2,1,0:T(8,128)(2,1)S(1)}, bf16[1,320,128]{2,1,0:T(8,128)(2,1)S(1)}, u32[]{:S(2)}, u32[]{:S(2)}) collective-permute-start(bf16[1,320,128]{2,1,0:T(8,128)(2,1)S(1)} %fusion.22), channel_id=1, source_target_pairs={{0,1},{1,2},{2,3},{4,5},{5,6},{6,7},{8,9},{9,10},{10,11},{12,13},{... | collective-permute-start | bytes 245768 | tf_op jit(solution)/shard_map/ppermute | solution.py:22
  15.0 1.0 convert_reduce_fusion
  17.5 1.0 constant_dynamic-update-slice_fusion.1
  19.4 3.3 %gather_fusion = bf16[336,2880]{1,0:T(8,128)(2,1)} fusion(bf16[320,2880]{1,0:T(8,128)(2,1)S(1)} %convolution_bitcast_fusion, s32[1024]{0:T(1024)S(1)} %pad_clamp_fusion.1), kind=kCustom, calls=%fused_computation | custom fusion | bytes 3872064 | tf_op jit(solution)/shard_map/jit(_take)/gather | solution.py:106
  22.8 1.9 %gather.10 = bf16[8,42,2880]{2,1,0:T(8,128)(2,1)S(1)} reshape(bf16[336,2880]{1,0:T(8,128)(2,1)} %gather_fusion) | data formatting | bytes 3870720 | tf_op jit(solution)/shard_map/jit(_take)/gather | solution.py:106
  25.3 32.3 %all_to_all.5 = bf16[8,42,2880]{2,1,0:T(8,128)(2,1)S(1)} all-to-all(bf16[8,42,2880]{2,1,0:T(8,128)(2,1)S(1)} %select_convert_fusion), channel_id=1, replica_groups=mesh['dp'=8,'strip'=4] {'dp'}, dimensions={0} | all-to-all | bytes 3870720 | tf_op jit(solution)/shard_map/all_to_all | solution.py:109
  57.6 1.1 reduce_sum.32
  59.7 35.0 %all-reduce.4.cloned.1.call-done = bf16[42,2880]{1,0:T(8,128)(2,1)} async-done(((bf16[42,2880]{1,0:T(8,128)(2,1)}), bf16[42,2880]{1,0:T(8,128)(2,1)}) %all-reduce.4.cloned.1.call-update) | async-done | bytes 241936 | tf_op jit(solution)/shard_map/psum | solution.py:112
  94.6 3.3 %convert_bitcast_fusion = (bf16[1,42,2880]{2,1,0:T(8,128)(2,1)}, f32[42,2880]{1,0:T(8,128)}, f32[42,2880]{1,0:T(8,128)}, f32[42,2880]{1,0:T(8,128)}) fusion(f32[42,2880]{1,0:T(8,128)} %param.10, f32[42,2880]{1,0:T(8,128)} %param.12, bf16[42,2880]{1,0:T(8,128)(2,1)} %all-reduce.4.cloned.1.call-done, f32[42,2880]{1,0:T(8,128)} %param.11, ...), kind=kLoop, calls=%fused_computation.42 | loop fusion | flops 2177280 | bytes 3386922
  98.0 1.3 collective-permute-start.3
  99.3 4.6 %collective-permute-start.2 = (bf16[1,320,128]{2,1,0:T(8,128)(2,1)S(1)}, bf16[1,320,128]{2,1,0:T(8,128)(2,1)S(1)}, u32[]{:S(2)}, u32[]{:S(2)}) collective-permute-start(bf16[1,320,128]{2,1,0:T(8,128)(2,1)S(1)} %bitcast.60), channel_id=1, source_target_pairs={{0,1},{1,2},{2,3},{4,5},{5,6},{6,7},{8,9},{9,10},{10,11},{12,13},{... | collective-permute-start | bytes 245768 | tf_op jit(solution)/shard_map/ppermute | solution.py:22
  104.3 2.8 %collective-permute-done.2 = bf16[1,320,128]{2,1,0:T(8,128)(2,1)S(1)} collective-permute-done((bf16[1,320,128]{2,1,0:T(8,128)(2,1)S(1)}, bf16[1,320,128]{2,1,0:T(8,128)(2,1)S(1)}, u32[]{:S(2)}, u32[]{:S(2)}) %collective-permute-start.2) | collective-permute-done | bytes 81952 | tf_op jit(solution)/shard_map/ppermute | solution.py:22
  107.4 0.7 slice_dynamic-update-slice_fusion.5
  109.4 0.7 slice_dynamic-update-slice_fusion.3
  113.4 24.9 %all-gather.4.cloned.1.call-done = bf16[320,2880]{1,0:T(8,128)(2,1)} async-done(((bf16[80,2880]{1,0:T(8,128)(2,1)}), bf16[320,2880]{1,0:T(8,128)(2,1)}) %all-gather.4.cloned.1.call-update) | async-done | bytes 1843216 | tf_op jit(solution)/shard_map/all_gather | solution.py:74
  138.3 3.3 %copy.17 = bf16[320,2880]{0,1:T(8,128)(2,1)S(1)} copy(bf16[320,2880]{1,0:T(8,128)(2,1)} %all-gather.4.cloned.1.call-done) | data formatting | bytes 3686400 | tf_op jit(solution)/shard_map/all_gather | solution.py:74
  141.6 2.5 %copy.18 = bf16[320,9,320]{0,2,1:T(8,128)(2,1)} copy(bf16[320,9,320]{2,0,1:T(8,128)(2,1)S(1)} %bitcast.57) | data formatting | bytes 3686400 | tf_op jit(solution)/shard_map/transpose | solution.py:48
  144.1 3.0 %fusion.6 = bf16[1,1,320,128]{3,2,1,0:T(8,128)(2,1)} fusion(bf16[320,2880]{1,0:T(8,128)(2,1)} %all-gather.4.cloned.1.call-done, bf16[1,2880,128]{2,1,0:T(8,128)(2,1)S(1)} %slice_dynamic-update-slice_fusion.6, bf16[1,1,320,128]{3,2,1,0:T(8,128)(2,1)S(1)} %copy-done.2), kind=kOutput, calls=%fused_computation.14 | convolution fusion | flops 236052480 | bytes 2744320 | tf_op jit(solution)/shard_map/ok,hkw->how/dot_general | solution.py:82
  147.0 2.8 %fusion.5 = bf16[1,1,320,128]{3,2,1,0:T(8,128)(2,1)} fusion(bf16[320,2880]{0,1:T(8,128)(2,1)S(1)} %bitcast.58, bf16[1,2880,128]{2,1,0:T(8,128)(2,1)} %slice_dynamic-update-slice_fusion, bf16[1,1,320,128]{3,2,1,0:T(8,128)(2,1)S(1)} %copy-done.2, bf16[1,1,320,128]{3,2,1,0:T(8,128)(2,1)S(1)} %copy-done.1), kind=kOutput, calls=%fused_computation.13 | convolution fusion | flops 236421120 | bytes 2826240 | tf_op jit(solution)/shard_map/ck,hkw->hcw/dot_general | solution.py:88
  149.8 19.2 %all-gather.6.cloned.1.call-done = bf16[8,42,2880]{2,1,0:T(8,128)(2,1)} async-done(((bf16[1,42,2880]{2,1,0:T(8,128)(2,1)}), bf16[8,42,2880]{2,1,0:T(8,128)(2,1)}) %all-gather.6.cloned.1.call-update) | async-done | bytes 1935376 | tf_op jit(solution)/shard_map/all_gather | solution.py:122
  169.0 2.2 %reshape.171 = bf16[336,2880]{1,0:T(8,128)(2,1)S(1)} reshape(bf16[8,42,2880]{2,1,0:T(8,128)(2,1)} %all-gather.6.cloned.1.call-done) | data formatting | bytes 3870720
  171.2 1.6 gather_fusion.1
  (45 shorter events, 9.2 us)
Async XLA Ops:
  7.2 11.6 %copy-start.1 = (bf16[1,1,320,128]{3,2,1,0:T(8,128)(2,1)S(1)}, bf16[1,1,320,128]{3,2,1,0:T(8,128)(2,1)}, u32[]{:S(2)}) copy-start(bf16[1,1,320,128]{3,2,1,0:T(8,128)(2,1)} %param.8) | copy-start | bytes 245764
  7.2 87.4 %all-reduce.4.cloned.1.call-start = ((), (), s32[]{:S(2)}) async-start(), calls=%async_computation.2 | async-start | bytes 565248 | tf_op jit(solution)/shard_map/psum | solution.py:112
  8.2 8.9 %collective-permute-start.1 = (bf16[1,320,128]{2,1,0:T(8,128)(2,1)S(1)}, bf16[1,320,128]{2,1,0:T(8,128)(2,1)S(1)}, u32[]{:S(2)}, u32[]{:S(2)}) collective-permute-start(bf16[1,320,128]{2,1,0:T(8,128)(2,1)S(1)} %fusion.22), channel_id=1, source_target_pairs={{1,0},{2,1},{3,2},{5,4},{6,5},{7,6},{9,8},{10,9},{11,10},{13,12},{... | collective-permute-start | bytes 245768 | tf_op jit(solution)/shard_map/ppermute | solution.py:24
  9.5 7.7 %collective-permute-start = (bf16[1,320,128]{2,1,0:T(8,128)(2,1)S(1)}, bf16[1,320,128]{2,1,0:T(8,128)(2,1)S(1)}, u32[]{:S(2)}, u32[]{:S(2)}) collective-permute-start(bf16[1,320,128]{2,1,0:T(8,128)(2,1)S(1)} %fusion.22), channel_id=1, source_target_pairs={{0,1},{1,2},{2,3},{4,5},{5,6},{6,7},{8,9},{9,10},{10,11},{12,13},{... | collective-permute-start | bytes 245768 | tf_op jit(solution)/shard_map/ppermute | solution.py:22
  58.8 79.5 %all-gather.4.cloned.1.call-start = ((), (), s32[]{:S(2)}) async-start(), calls=%async_computation.1 | async-start | bytes 2355200 | tf_op jit(solution)/shard_map/all_gather | solution.py:74
  59.5 109.5 %all-gather.6.cloned.1.call-start = ((), (), s32[]{:S(2)}) async-start(), calls=%async_computation.3 | async-start | bytes 2543616 | tf_op jit(solution)/shard_map/all_gather | solution.py:122
  98.0 6.3 %collective-permute-start.3 = (bf16[1,320,128]{2,1,0:T(8,128)(2,1)S(1)}, bf16[1,320,128]{2,1,0:T(8,128)(2,1)S(1)}, u32[]{:S(2)}, u32[]{:S(2)}) collective-permute-start(bf16[1,320,128]{2,1,0:T(8,128)(2,1)S(1)} %bitcast.59), channel_id=1, source_target_pairs={{1,0},{2,1},{3,2},{5,4},{6,5},{7,6},{9,8},{10,9},{11,10},{13,12},{... | collective-permute-start | bytes 245768 | tf_op jit(solution)/shard_map/ppermute | solution.py:24
  99.3 7.9 %collective-permute-start.2 = (bf16[1,320,128]{2,1,0:T(8,128)(2,1)S(1)}, bf16[1,320,128]{2,1,0:T(8,128)(2,1)S(1)}, u32[]{:S(2)}, u32[]{:S(2)}) collective-permute-start(bf16[1,320,128]{2,1,0:T(8,128)(2,1)S(1)} %bitcast.60), channel_id=1, source_target_pairs={{0,1},{1,2},{2,3},{4,5},{5,6},{6,7},{8,9},{9,10},{10,11},{12,13},{... | collective-permute-start | bytes 245768 | tf_op jit(solution)/shard_map/ppermute | solution.py:22
  141.6 2.5 %copy-start.2 = (bf16[1,1,320,128]{3,2,1,0:T(8,128)(2,1)S(1)}, bf16[1,1,320,128]{3,2,1,0:T(8,128)(2,1)}, u32[]{:S(2)}) copy-start(bf16[1,1,320,128]{3,2,1,0:T(8,128)(2,1)} %param.7) | copy-start | bytes 245764
  144.1 3.0 %copy-start = (bf16[320,9,320]{0,2,1:T(8,128)(2,1)S(1)}, bf16[320,9,320]{0,2,1:T(8,128)(2,1)}, u32[]{:S(2)}) copy-start(bf16[320,9,320]{0,2,1:T(8,128)(2,1)} %copy.18) | copy-start | bytes 5529604
Sparse Core Ops, SparseCore 0:
  58.9 35.6 all-reduce.3
  96.2 42.0 all-gather.3
  140.7 28.2 all-gather.5
where the time goes:
time: 180 us; the launch traced here: 179 us
  waiting for transfers between devices  83 us (46%)
  blocking collectives  32.3 us (18%)
  local copies, waits for them, and re-layouts  21.4 us (12%)
  between operations  14 us (8%)
  starting transfers between devices  12.8 us (7%)
  other arithmetic  9.54 us (5%)
  matrix products  6.37 us (4%)
    psum x1, waiting for transfers between devices, local(): lax.psum(jnp.sum(incoming, axis=0).astype(jnp.bfloat16), 'strip')  35 us
    all_to_all x1, blocking collectives, local(): lax.all_to_all(outgoing.astype(jnp.bfloat16), 'dp', split_axis=0, concat_...  32.3 us
    all_gather x1, waiting for transfers between devices, local(): full_weight = lax.all_gather(weight, 'strip', axis=0, tiled=True)  24.9 us
    all_gather x1, waiting for transfers between devices, local(): lax.all_gather(new_master.astype(jnp.bfloat16), 'dp', axis=0, tiled=True)  19.2 us
    ppermute x2, starting transfers between devices, extended(): lax.ppermute(tail, axis, [(i, (i + 1) % count) for i in range(ends)])  10.1 us
    unnamed x22, local copies, waits for them, and re-layouts  7.87 us
    gather x2, local copies, waits for them, and re-layouts, local(): jnp.take(partial_grad, source_row, axis=0, mode='fill', fill_value=0.0)  5.2 us
    unnamed x2, other arithmetic  4.29 us
  transfers between devices with their start and end apart: 7, of which 5 were waited for; matrix products, arithmetic and copies ran while one was open for 13% of the time, Pallas kernels for 0%

commit v1 on v0

v1 whole, which is shorter than its diff:
```python
import functools
import math

import jax
import jax.numpy as jnp
from jax import lax
from jax.experimental import pallas as pl
from jax.experimental.pallas import tpu as pltpu
from jax.sharding import PartitionSpec as P

beta_first = 0.9
beta_second = 0.999
learn_rate = 0.01
epsilon = 1e-08
bias_first = 1.0 - 0.9**10
bias_second = 1.0 - 0.999**10

MESH = pl.DeviceIdType.MESH
bf16 = jnp.bfloat16
f32 = jnp.float32


def shifted(x, step, wid):
    if step == 0:
        return x
    lane = lax.broadcasted_iota(jnp.int32, x.shape, 1) % wid
    moved = pltpu.roll(x, (-step) % x.shape[1], 1)
    return jnp.where(lane == (wid - 1 if step > 0 else 0), 0.0, moved)


def fill_cols(x, out_ref, wid):
    chans, total = x.shape
    zero = jnp.zeros((chans, wid), bf16)
    for dw in (-1, 0, 1):
        moved = shifted(x, dw, wid).astype(bf16)
        padded = jnp.concatenate([zero, moved, zero], axis=1)
        for dh in (-1, 0, 1):
            tap = 3 * (dh + 1) + dw + 1
            out_ref[tap * chans : (tap + 1) * chans, :] = padded[:, (1 + dh) * wid : (1 + dh) * wid + total]


def kernel(
    dp, ns, cap, capp,
    lat_ref, cot_ref, w_ref, master_ref, first_ref, second_ref, own_col, own_row,
    out_ref, gin_ref, nw_ref, nm_ref, nf_ref, nsec_ref,
    act_all, cot_all, cotp, actq, actg, cotg, cols, qcols, z_scr, conv_s, conv_r, spread_s, spread_r,
    gq, gacc, pub, slot_scr,
    s_act, r_act, s_cot, r_cot, s_aq, r_aq, s_cp, r_cp, s_cv, r_cv, s_sp, r_sp, s_g, r_g, s_pub, r_pub, s_fw,
):
    d = lax.axis_index("dp")
    s = lax.axis_index("strip")
    chans, wid = lat_ref.shape[2], lat_ref.shape[3]
    part = chans // ns
    sibling = d + 1 - 2 * lax.rem(d, 2)
    mine = pl.ds(pl.multiple_of(s * part, part), part)

    def copy(src, dst, ss, rs, to):
        return pltpu.make_async_remote_copy(
            src_ref=src, dst_ref=dst, send_sem=ss, recv_sem=rs, device_id=to, device_id_type=MESH
        )

    def strip_peer(i):
        return lax.rem(s + i, ns)

    def dp_peer(i):
        return lax.rem(d + i, dp)

    barrier = pltpu.get_barrier_semaphore()
    for i in range(1, ns):
        pl.semaphore_signal(barrier, inc=1, device_id=(d, strip_peer(i)), device_id_type=MESH)

    def greet(i, c):
        pl.semaphore_signal(barrier, inc=1, device_id=(dp_peer(i), s), device_id_type=MESH)
        return c

    lax.fori_loop(1, dp, greet, 0)
    pix = lat_ref[0, 0].astype(f32)
    sig = 1.0 / (1.0 + jnp.exp(-pix))
    act_all[s] = (pix * sig).astype(bf16)
    cot_all[s] = cot_ref[0, 0]
    pl.semaphore_wait(barrier, ns - 1 + dp - 1)

    def act_copy(i, block):
        return copy(act_all.at[block], act_all.at[block], s_act.at[i], r_act.at[block], (d, strip_peer(i)))

    def cot_copy(i, block):
        return copy(cot_all.at[block], cot_all.at[block], s_cot.at[i], r_cot.at[block], (d, strip_peer(i)))

    for i in range(1, ns):
        cot_copy(i, s).start()
    for i in range(1, ns):
        act_copy(i, s).start()

    oc = own_col[...]
    orow = own_row[...]
    a0 = lax.broadcasted_iota(jnp.int32, (chans, chans), 0)
    a1 = lax.broadcasted_iota(jnp.int32, (chans, chans), 1)
    same = oc == orow
    within_row = jnp.sum(jnp.where(same & (a0 < a1), 1.0, 0.0), axis=0, keepdims=True).astype(jnp.int32)
    within_col = jnp.sum(jnp.where(same & (a1 < a0), 1.0, 0.0), axis=1, keepdims=True).astype(jnp.int32)
    slot_row = orow * capp + within_row
    slot_scr[...] = oc * capp + within_col
    owned = jnp.sum(jnp.where(orow == d, 1.0, 0.0), axis=1, keepdims=True)
    keep = lax.broadcasted_iota(jnp.int32, (cap, 1), 0).astype(f32) < owned
    pick = jnp.where(
        lax.broadcasted_iota(jnp.int32, (dp * capp, chans), 0) == slot_row, 1.0, 0.0
    ).astype(bf16)

    for i in range(1, ns):
        cot_copy(i, strip_peer(i)).wait_recv()
    for row in range(ns):
        chosen = jnp.dot(pick, cot_all[row], preferred_element_type=f32).astype(bf16)
        cotp[:, :, row * wid : (row + 1) * wid] = chosen.reshape(dp, capp, wid)

    def cp_copy(j, block):
        return copy(cotp.at[j], cotg.at[block], s_cp.at[j], r_cp.at[block], (j, s))

    def send_cp(i, c):
        cp_copy(dp_peer(i), d).start()
        return c

    lax.fori_loop(1, dp, send_cp, 0)
    cotg[d] = cotp[d]

    for i in range(1, ns):
        act_copy(i, strip_peer(i)).wait_recv()
    for row in range(ns):
        actq[:, row * wid : (row + 1) * wid] = act_all[row, mine, :]

    def aq_copy(j, block):
        return copy(actq, actg.at[block], s_aq.at[j], r_aq.at[block], (j, s))

    def send_aq(i, c):
        aq_copy(dp_peer(i), d).start()
        return c

    lax.fori_loop(1, dp, send_aq, 0)
    actg[d] = actq[...]

    whole = jnp.concatenate([act_all[row] for row in range(ns)], axis=1).astype(f32)
    fill_cols(whole, cols, wid)
    conv = jnp.dot(w_ref[...], cols[...], preferred_element_type=f32)
    for row in range(ns):
        conv_s[row] = conv[:, row * wid : (row + 1) * wid].astype(bf16)

    def cv_copy(i, block):
        return copy(conv_s.at[strip_peer(i)], conv_r.at[block], s_cv.at[i], r_cv.at[block], (d, strip_peer(i)))

    upq = jnp.concatenate([cot_all[row, mine, :] for row in range(ns)], axis=1)
    z_scr[...] = lax.dot_general(w_ref[...], upq, (((0,), (0,)), ((), ())), preferred_element_type=f32)
    zero = jnp.zeros((chans, wid), f32)
    spread = None
    for dw in (-1, 0, 1):
        total = None
        for dh in (-1, 0, 1):
            tap = 3 * (dh + 1) + dw + 1
            piece = z_scr[tap * chans : (tap + 1) * chans, :]
            if dh == 1:
                piece = jnp.concatenate([zero, piece[:, : (ns - 1) * wid]], axis=1)
            if dh == -1:
                piece = jnp.concatenate([piece[:, wid:], zero], axis=1)
            total = piece if total is None else total + piece
        total = shifted(total, -dw, wid)
        spread = total if spread is None else spread + total
    for row in range(ns):
        spread_s[row] = spread[:, row * wid : (row + 1) * wid].astype(bf16)

    def sp_copy(i, block):
        return copy(spread_s.at[strip_peer(i)], spread_r.at[block], s_sp.at[i], r_sp.at[block], (d, strip_peer(i)))

    gacc[...] = jnp.zeros_like(gacc)

    def grad_of(j):
        fill_cols(actg[j].astype(f32), qcols, wid)
        gacc[...] += lax.dot_general(
            cotg[j], qcols[...], (((1,), (1,)), ((), ())), preferred_element_type=f32
        )

    grad_of(d)

    def grad_step(i, c):
        j = dp_peer(i)
        cp_copy(j, j).wait_recv()
        aq_copy(j, j).wait_recv()
        grad_of(j)
        return c

    lax.fori_loop(1, dp, grad_step, 0)
    gq[s] = (gacc[...] * (1.0 / math.sqrt(dp * ns * wid))).astype(bf16)

    def g_copy(i, block):
        return copy(gq.at[block], gq.at[block], s_g.at[i], r_g.at[block], (d, strip_peer(i)))

    for i in range(1, ns):
        g_copy(i, s).start()
    for i in range(1, ns):
        cv_copy(i, s).start()
        sp_copy(i, s).start()
    for i in range(1, ns):
        g_copy(i, strip_peer(i)).wait_recv()
    pieces = []
    for tap in range(9):
        for row in range(ns):
            pieces.append(gq[row, :, tap * part : (tap + 1) * part])
    grads = jnp.concatenate(pieces, axis=1).astype(f32)[:cap]
    first = first_ref[...]
    second = second_ref[...]
    master = master_ref[...]
    first_new = beta_first * first + (1.0 - beta_first) * grads
    second_new = beta_second * second + (1.0 - beta_second) * grads * grads
    update = learn_rate * (first_new / bias_first) / (jnp.sqrt(second_new / bias_second) + epsilon)
    master_new = jnp.where(keep, master - update, master)
    nm_ref[...] = master_new
    nf_ref[...] = jnp.where(keep, first_new, first)
    nsec_ref[...] = jnp.where(keep, second_new, second)
    pub[d] = jnp.concatenate(
        [master_new, jnp.zeros((capp - cap, master_new.shape[1]), f32)], axis=0
    ).astype(bf16)

    def pub_copy(i, j, block):
        return copy(pub.at[block], pub.at[block], s_pub.at[i], r_pub.at[block], (j, s))

    def fw_copy(block):
        return copy(pub.at[block], pub.at[block], s_fw.at[block], r_pub.at[block], (sibling, s))

    half = dp // 2

    def send_pub(i, c):
        pub_copy(i, dp_peer(2 * i), d).start()
        return c

    lax.fori_loop(1, half, send_pub, 0)
    fw_copy(d).start()

    for i in range(1, ns):
        cv_copy(i, strip_peer(i)).wait_recv()
        sp_copy(i, strip_peer(i)).wait_recv()
    conv_r[s] = conv_s[s]
    spread_r[s] = spread_s[s]
    pix = lat_ref[0, 0].astype(f32)
    sig = 1.0 / (1.0 + jnp.exp(-pix))
    out_ref[0, 0] = (pix + conv_r[...].reshape(chans, wid).astype(f32)).astype(bf16)
    back = spread_r[0].astype(f32)
    for row in range(1, ns):
        back = back + spread_r[row].astype(f32)
    gin_ref[0, 0] = (
        cot_ref[0, 0].astype(f32) + back * (sig * (1.0 + pix * (1.0 - sig)))
    ).astype(bf16)

    def forward(i, c):
        j = dp_peer(2 * i)
        pub_copy(i, j, j).wait_recv()
        fw_copy(j).start()
        return c

    lax.fori_loop(1, half, forward, 0)
    base = sibling

    def arrive(i, c):
        fw_copy(lax.rem(base + 2 * i, dp)).wait_recv()
        return c

    lax.fori_loop(0, half, arrive, 0)
    slots = slot_scr[mine, :]
    want = jnp.where(
        lax.broadcasted_iota(jnp.int32, (part, dp * capp), 1) == slots, 1.0, 0.0
    ).astype(bf16)
    nw_ref[...] = jnp.dot(
        want, pub[...].reshape(dp * capp, pub.shape[2]), preferred_element_type=f32
    ).astype(bf16)

    for i in range(1, ns):
        act_copy(i, s).wait_send()
        cot_copy(i, s).wait_send()
        cv_copy(i, s).wait_send()
        sp_copy(i, s).wait_send()
        g_copy(i, s).wait_send()

    def left(i, c):
        j = dp_peer(i)
        cp_copy(j, d).wait_send()
        aq_copy(j, d).wait_send()
        return c

    lax.fori_loop(1, dp, left, 0)

    def left_pub(i, c):
        pub_copy(i, dp_peer(2 * i), d).wait_send()
        fw_copy(dp_peer(2 * i)).wait_send()
        return c

    lax.fori_loop(1, half, left_pub, 0)
    fw_copy(d).wait_send()


def local(dp, ns, latents, cotangent, weight, master, first_moment, second_moment, owner_list):
    chans, wid = latents.shape[2], latents.shape[3]
    cap = master.shape[0]
    capp = -(-cap // 16) * 16
    part = chans // ns
    width = weight.shape[1]
    pixels = ns * wid
    dma = lambda n: pltpu.SemaphoreType.DMA((n,))
    vmem = pl.BlockSpec(memory_space=pltpu.VMEM)
    arrays = (latents, cotangent, weight, master, first_moment, second_moment)
    scratch = [
        pltpu.VMEM((ns, chans, wid), bf16),
        pltpu.VMEM((ns, chans, wid), bf16),
        pltpu.VMEM((dp, capp, pixels), bf16),
        pltpu.VMEM((part, pixels), bf16),
        pltpu.VMEM((dp, part, pixels), bf16),
        pltpu.VMEM((dp, capp, pixels), bf16),
        pltpu.VMEM((9 * chans, pixels), bf16),
        pltpu.VMEM((9 * part, pixels), bf16),
        pltpu.VMEM((9 * chans, pixels), f32),
        pltpu.VMEM((ns, part, wid), bf16),
        pltpu.VMEM((ns, part, wid), bf16),
        pltpu.VMEM((ns, chans, wid), bf16),
        pltpu.VMEM((ns, chans, wid), bf16),
        pltpu.VMEM((ns, capp, 9 * part), bf16),
        pltpu.VMEM((capp, 9 * part), f32),
        pltpu.VMEM((dp, capp, width), bf16),
        pltpu.VMEM((chans, 1), jnp.int32),
    ] + [dma(n) for n in (ns, ns, ns, ns, dp, dp, dp, dp, ns, ns, ns, ns, ns, ns, dp, dp, dp)]
    return tuple(
        pl.pallas_call(
            functools.partial(kernel, dp, ns, cap, capp),
            out_shape=[
                jax.ShapeDtypeStruct(a.shape, a.dtype)
                for a in (latents, cotangent, weight, master, first_moment, second_moment)
            ],
            in_specs=[vmem] * 8,
            out_specs=[vmem] * 6,
            scratch_shapes=scratch,
            compiler_params=pltpu.CompilerParams(
                collective_id=0, has_side_effects=True, vmem_limit_bytes=58 * 2**20
            ),
            cost_estimate=pl.CostEstimate(flops=10**9, bytes_accessed=6 * 10**6, transcendentals=10**5),
        )(*arrays, owner_list.reshape(chans, 1), owner_list.reshape(1, chans))
    )


def solution(mesh):
    image = P("dp", "strip", None, None)
    state = P("dp", None)
    in_specs = (image, image, P("strip", None), state, state, state, P())
    out_specs = (image, image, P("strip", None), state, state, state)
    fn = functools.partial(local, mesh.shape["dp"], mesh.shape["strip"])
    return jax.shard_map(fn, mesh=mesh, in_specs=in_specs, out_specs=out_specs, check_vma=False)
```

time: 180 us -> 74.7 us (0.42)
  the two profiles are of different devices: /device:TPU:0 before, /device:TPU:29 now
where the time goes in v1:
time: 74.7 us; the launch traced here: 74.4 us
  Pallas kernels  64.3 us (86%)
  local copies, waits for them, and re-layouts  9.44 us (13%)
    pallas_call x1, Pallas kernels, local(): pl.pallas_call(functools.partial(kernel, dp, ns, cap, capp), out_shape=[j...  64.3 us
    unnamed x16, local copies, waits for them, and re-layouts  7.36 us

profile of v1, /device:TPU:29, one launch (start us, length us, event | category | flops | bytes accessed | tf_op | source)
XLA Modules:
  0.0 74.4 jit_solution(4242706092487510023)
XLA Ops:
  0.6 0.0 copy-start.4
  0.6 1.3 %reshape.19.own_row = s32[1,320]{1,0:T(1,128)} reshape(s32[320]{0:T(512)} %param.13) | data formatting | bytes 2560 | tf_op jit(solution)/shard_map/reshape | solution.py:339
  2.0 0.0 copy-done.4
  2.0 0.8 %reshape.20.own_col = s32[320,1]{1,0:T(8,128)} reshape(s32[320]{0:T(512)S(1)} %copy-done.4) | data formatting | bytes 2560 | tf_op jit(solution)/shard_map/reshape | solution.py:339
  2.7 64.3 %shard_map.118 = (bf16[1,1,320,128]{3,2,1,0:T(8,128)(2,1)}, bf16[1,1,320,128]{3,2,1,0:T(8,128)(2,1)}, bf16[80,2880]{1,0:T(8,128)(2,1)}, f32[42,2880]{1,0:T(8,128...) custom-call(bf16[1,1,320,128]{3,2,1,0:T(8,128)(2,1)} %lat_ref.1, bf16[1,1,320,128]{3,2,1,0:T(8,128)(2,1)} %cot_ref.1, ...), custom_call_target="tpu_custom_call" | custom-call | flops 1000000000 | bytes 6000000 | tf_op jit(solution)/shard_map/pallas_call | solution.py:326
  67.0 0.0 copy-start.3
  67.0 1.6 %copy.20 = bf16[1,1,320,128]{3,2,1,0:T(8,128)(2,1)} copy(bf16[1,1,320,128]{3,2,1,0:T(8,128)(2,1)} %get-tuple-element.12) | data formatting | bytes 163840
  68.6 0.0 copy-done.3
  68.6 0.0 copy-start.2
  68.6 0.6 copy.21
  69.2 1.8 %copy.22 = bf16[80,2880]{1,0:T(8,128)(2,1)} copy(bf16[80,2880]{1,0:T(8,128)(2,1)} %get-tuple-element.14) | data formatting | bytes 921600
  71.1 0.0 copy-done.2
  71.1 0.0 copy-start.1
  71.1 0.8 %copy.23 = f32[42,2880]{1,0:T(8,128)} copy(f32[42,2880]{1,0:T(8,128)S(1)} %copy-done.2) | data formatting | bytes 967680
  71.9 0.5 copy-done.1
  72.3 0.0 copy-start
  72.3 0.8 %copy.24 = f32[42,2880]{1,0:T(8,128)} copy(f32[42,2880]{1,0:T(8,128)S(1)} %copy-done.1) | data formatting | bytes 967680
  73.1 0.5 copy-done
  73.6 0.8 %copy.25 = f32[42,2880]{1,0:T(8,128)} copy(f32[42,2880]{1,0:T(8,128)S(1)} %copy-done) | data formatting | bytes 967680
Async XLA Ops:
  0.6 1.3 %copy-start.4 = (s32[320]{0:T(512)S(1)}, s32[320]{0:T(512)}, u32[]{:S(2)}) copy-start(s32[320]{0:T(512)} %param.13) | copy-start | bytes 3844
  67.0 1.6 %copy-start.3 = (bf16[1,1,320,128]{3,2,1,0:T(8,128)(2,1)S(1)}, bf16[1,1,320,128]{3,2,1,0:T(8,128)(2,1)}, u32[]{:S(2)}) copy-start(bf16[1,1,320,128]{3,2,1,0:T(8,128)(2,1)} %get-tuple-element.13) | copy-start | bytes 245764
  68.6 2.5 %copy-start.2 = (f32[42,2880]{1,0:T(8,128)S(1)}, f32[42,2880]{1,0:T(8,128)}, u32[]{:S(2)}) copy-start(f32[42,2880]{1,0:T(8,128)} %get-tuple-element.15) | copy-start | bytes 1451524
  71.1 1.3 %copy-start.1 = (f32[42,2880]{1,0:T(8,128)S(1)}, f32[42,2880]{1,0:T(8,128)}, u32[]{:S(2)}) copy-start(f32[42,2880]{1,0:T(8,128)} %get-tuple-element.16) | copy-start | bytes 1451524
  72.3 1.3 %copy-start = (f32[42,2880]{1,0:T(8,128)S(1)}, f32[42,2880]{1,0:T(8,128)}, u32[]{:S(2)}) copy-start(f32[42,2880]{1,0:T(8,128)} %get-tuple-element.17) | copy-start | bytes 1451524

commit v2 on v1

--- a/solution.py
+++ b/solution.py
@@ -41,11 +41,12 @@
 
 def kernel(
     dp, ns, cap, capp,
-    lat_ref, cot_ref, w_ref, master_ref, first_ref, second_ref, own_col, own_row,
-    out_ref, gin_ref, nw_ref, nm_ref, nf_ref, nsec_ref,
+    lat_ref, cot_ref, w_hbm, master_hbm, first_hbm, second_hbm, own_ref,
+    out_ref, gin_ref, nw_ref, nm_hbm, nf_hbm, nsec_hbm,
+    w_ref, master_ref, first_ref, second_ref, nm_ref, nf_ref, nsec_ref, actz,
     act_all, cot_all, cotp, actq, actg, cotg, cols, qcols, z_scr, conv_s, conv_r, spread_s, spread_r,
     gq, gacc, pub, slot_scr,
-    s_act, r_act, s_cot, r_cot, s_aq, r_aq, s_cp, r_cp, s_cv, r_cv, s_sp, r_sp, s_g, r_g, s_pub, r_pub, s_fw,
+    s_act, r_act, s_cot, r_cot, s_aq, r_aq, s_cp, r_cp, s_cv, r_cv, s_sp, r_sp, s_g, r_g, s_pub, r_pub, s_fw, s_az, r_az, s_in, s_out,
 ):
     d = lax.axis_index("dp")
     s = lax.axis_index("strip")
@@ -54,6 +55,15 @@
     sibling = d + 1 - 2 * lax.rem(d, 2)
     mine = pl.ds(pl.multiple_of(s * part, part), part)
 
+    loads = [
+        pltpu.make_async_copy(src, dst, s_in.at[k])
+        for k, (src, dst) in enumerate(
+            ((w_hbm, w_ref), (master_hbm, master_ref), (first_hbm, first_ref), (second_hbm, second_ref))
+        )
+    ]
+    for load in loads:
+        load.start()
+
     def copy(src, dst, ss, rs, to):
         return pltpu.make_async_remote_copy(
             src_ref=src, dst_ref=dst, send_sem=ss, recv_sem=rs, device_id=to, device_id_type=MESH
@@ -78,6 +88,7 @@
     sig = 1.0 / (1.0 + jnp.exp(-pix))
     act_all[s] = (pix * sig).astype(bf16)
     cot_all[s] = cot_ref[0, 0]
+    actz[s] = act_all[s, mine, :]
     pl.semaphore_wait(barrier, ns - 1 + dp - 1)
 
     def act_copy(i, block):
@@ -88,13 +99,17 @@
 
     for i in range(1, ns):
         cot_copy(i, s).start()
-    for i in range(1, ns):
-        act_copy(i, s).start()
-
-    oc = own_col[...]
-    orow = own_row[...]
+    def az_copy(i, block):
+        rows = pl.ds(pl.multiple_of(strip_peer(i) * part, part), part)
+        return copy(act_all.at[s, rows, :], actz.at[block], s_az.at[i], r_az.at[block], (d, strip_peer(i)))
+
+    for i in range(1, ns):
+        az_copy(i, s).start()
+
+    orow = own_ref[...].reshape(1, chans)
     a0 = lax.broadcasted_iota(jnp.int32, (chans, chans), 0)
     a1 = lax.broadcasted_iota(jnp.int32, (chans, chans), 1)
+    oc = jnp.sum(jnp.where(a0 == a1, orow.astype(f32), 0.0), axis=1, keepdims=True).astype(jnp.int32)
     same = oc == orow
     within_row = jnp.sum(jnp.where(same & (a0 < a1), 1.0, 0.0), axis=0, keepdims=True).astype(jnp.int32)
     within_col = jnp.sum(jnp.where(same & (a1 < a0), 1.0, 0.0), axis=1, keepdims=True).astype(jnp.int32)
@@ -123,9 +138,9 @@
     cotg[d] = cotp[d]
 
     for i in range(1, ns):
-        act_copy(i, strip_peer(i)).wait_recv()
+        az_copy(i, strip_peer(i)).wait_recv()
     for row in range(ns):
-        actq[:, row * wid : (row + 1) * wid] = act_all[row, mine, :]
+        actq[:, row * wid : (row + 1) * wid] = actz[row]
 
     def aq_copy(j, block):
         return copy(actq, actg.at[block], s_aq.at[j], r_aq.at[block], (j, s))
@@ -137,15 +152,10 @@
     lax.fori_loop(1, dp, send_aq, 0)
     actg[d] = actq[...]
 
-    whole = jnp.concatenate([act_all[row] for row in range(ns)], axis=1).astype(f32)
-    fill_cols(whole, cols, wid)
-    conv = jnp.dot(w_ref[...], cols[...], preferred_element_type=f32)
-    for row in range(ns):
-        conv_s[row] = conv[:, row * wid : (row + 1) * wid].astype(bf16)
-
-    def cv_copy(i, block):
-        return copy(conv_s.at[strip_peer(i)], conv_r.at[block], s_cv.at[i], r_cv.at[block], (d, strip_peer(i)))
-
+    for i in range(1, ns):
+        act_copy(i, s).start()
+
+    loads[0].wait()
     upq = jnp.concatenate([cot_all[row, mine, :] for row in range(ns)], axis=1)
     z_scr[...] = lax.dot_general(w_ref[...], upq, (((0,), (0,)), ((), ())), preferred_element_type=f32)
     zero = jnp.zeros((chans, wid), f32)
@@ -194,10 +204,23 @@
     for i in range(1, ns):
         g_copy(i, s).start()
     for i in range(1, ns):
+        act_copy(i, strip_peer(i)).wait_recv()
+    whole = jnp.concatenate([act_all[row] for row in range(ns)], axis=1).astype(f32)
+    fill_cols(whole, cols, wid)
+    conv = jnp.dot(w_ref[...], cols[...], preferred_element_type=f32)
+    for row in range(ns):
+        conv_s[row] = conv[:, row * wid : (row + 1) * wid].astype(bf16)
+
+    def cv_copy(i, block):
+        return copy(conv_s.at[strip_peer(i)], conv_r.at[block], s_cv.at[i], r_cv.at[block], (d, strip_peer(i)))
+
+    for i in range(1, ns):
+        g_copy(i, strip_peer(i)).wait_recv()
+    for i in range(1, ns):
         cv_copy(i, s).start()
         sp_copy(i, s).start()
-    for i in range(1, ns):
-        g_copy(i, strip_peer(i)).wait_recv()
+    for load in loads[1:]:
+        load.wait()
     pieces = []
     for tap in range(9):
         for row in range(ns):
@@ -231,6 +254,12 @@
 
     lax.fori_loop(1, half, send_pub, 0)
     fw_copy(d).start()
+    stores = [
+        pltpu.make_async_copy(src, dst, s_out.at[k])
+        for k, (src, dst) in enumerate(((nm_ref, nm_hbm), (nf_ref, nf_hbm), (nsec_ref, nsec_hbm)))
+    ]
+    for store in stores:
+        store.start()
 
     for i in range(1, ns):
         cv_copy(i, strip_peer(i)).wait_recv()
@@ -269,7 +298,10 @@
         want, pub[...].reshape(dp * capp, pub.shape[2]), preferred_element_type=f32
     ).astype(bf16)
 
-    for i in range(1, ns):
+    for store in stores:
+        store.wait()
+    for i in range(1, ns):
+        az_copy(i, s).wait_send()
         act_copy(i, s).wait_send()
         cot_copy(i, s).wait_send()
         cv_copy(i, s).wait_send()
@@ -291,6 +323,15 @@
 
     lax.fori_loop(1, half, left_pub, 0)
     fw_copy(d).wait_send()
+
+
+def hand_over(*refs):
+    sems = refs[12]
+    copies = [pltpu.make_async_copy(refs[k], refs[6 + k], sems.at[k]) for k in range(6)]
+    for c in copies:
+        c.start()
+    for c in copies:
+        c.wait()
 
 
 def local(dp, ns, latents, cotangent, weight, master, first_moment, second_moment, owner_list):
@@ -303,7 +344,10 @@
     dma = lambda n: pltpu.SemaphoreType.DMA((n,))
     vmem = pl.BlockSpec(memory_space=pltpu.VMEM)
     arrays = (latents, cotangent, weight, master, first_moment, second_moment)
-    scratch = [
+    anywhere = pl.BlockSpec(memory_space=pl.ANY)
+    state = [pltpu.VMEM(master.shape, f32)] * 3
+    scratch = [pltpu.VMEM(weight.shape, bf16)] + state + state + [
+        pltpu.VMEM((ns, part, wid), bf16),
         pltpu.VMEM((ns, chans, wid), bf16),
         pltpu.VMEM((ns, chans, wid), bf16),
         pltpu.VMEM((dp, capp, pixels), bf16),
@@ -321,23 +365,29 @@
         pltpu.VMEM((capp, 9 * part), f32),
         pltpu.VMEM((dp, capp, width), bf16),
         pltpu.VMEM((chans, 1), jnp.int32),
-    ] + [dma(n) for n in (ns, ns, ns, ns, dp, dp, dp, dp, ns, ns, ns, ns, ns, ns, dp, dp, dp)]
-    return tuple(
-        pl.pallas_call(
+    ] + [dma(n) for n in (ns, ns, ns, ns, dp, dp, dp, dp, ns, ns, ns, ns, ns, ns, dp, dp, dp, ns, ns, 4, 3)]
+    made = pl.pallas_call(
             functools.partial(kernel, dp, ns, cap, capp),
             out_shape=[
                 jax.ShapeDtypeStruct(a.shape, a.dtype)
                 for a in (latents, cotangent, weight, master, first_moment, second_moment)
             ],
-            in_specs=[vmem] * 8,
-            out_specs=[vmem] * 6,
+            in_specs=[vmem] * 2 + [anywhere] * 4 + [vmem],
+            out_specs=[vmem] * 3 + [anywhere] * 3,
             scratch_shapes=scratch,
             compiler_params=pltpu.CompilerParams(
                 collective_id=0, has_side_effects=True, vmem_limit_bytes=58 * 2**20
             ),
             cost_estimate=pl.CostEstimate(flops=10**9, bytes_accessed=6 * 10**6, transcendentals=10**5),
-        )(*arrays, owner_list.reshape(chans, 1), owner_list.reshape(1, chans))
-    )
+        )(*arrays, owner_list)
+    results = pl.pallas_call(
+        hand_over,
+        out_shape=[jax.ShapeDtypeStruct(a.shape, a.dtype) for a in arrays],
+        in_specs=[anywhere] * 6,
+        out_specs=[anywhere] * 6,
+        scratch_shapes=[pltpu.SemaphoreType.DMA((6,))],
+    )(*made)
+    return tuple(results)
 
 
 def solution(mesh):

time: 74.7 us -> 129 us (1.73)
  the two profiles are of different devices: /device:TPU:29 before, /device:TPU:0 now
where the time goes in v2:
time: 129 us; the launch traced here: 128 us
  Pallas kernels  128 us (99%)
    pallas_call x1, Pallas kernels, local(): pl.pallas_call(hand_over, out_shape=[jax.ShapeDtypeStruct(a.shape, a.dtyp...  71.8 us
    pallas_call x1, Pallas kernels, local(): pl.pallas_call(functools.partial(kernel, dp, ns, cap, capp), out_shape=[j...  55.8 us

profile of v2, /device:TPU:0, one launch (start us, length us, event | category | flops | bytes accessed | tf_op | source)
XLA Modules:
  0.0 128.2 jit_solution(2089545927194094716)
XLA Ops:
  0.6 55.8 %shard_map.118 = (bf16[1,1,320,128]{3,2,1,0:T(8,128)(2,1)}, bf16[1,1,320,128]{3,2,1,0:T(8,128)(2,1)}, bf16[80,2880]{1,0:T(8,128)(2,1)}, f32[42,2880]{1,0:T(8,128...) custom-call(bf16[1,1,320,128]{3,2,1,0:T(8,128)(2,1)} %lat_ref.1, bf16[1,1,320,128]{3,2,1,0:T(8,128)(2,1)} %cot_ref.1, ...), custom_call_target="tpu_custom_call" | custom-call | flops 1000000000 | bytes 6000000 | tf_op jit(solution)/shard_map/pallas_call | solution.py:369
  56.4 71.8 %shard_map.119 = (bf16[1,1,320,128]{3,2,1,0:T(8,128)(2,1)}, bf16[1,1,320,128]{3,2,1,0:T(8,128)(2,1)}, bf16[80,2880]{1,0:T(8,128)(2,1)}, f32[42,2880]{1,0:T(8,128...) custom-call(bf16[1,1,320,128]{3,2,1,0:T(8,128)(2,1)} %get-tuple-element.12.refs_0_, ...), custom_call_target="tpu_custom_call" | custom-call | tf_op jit(solution)/shard_map/pallas_call | solution.py:383

commit v3 on v2

--- a/solution.py
+++ b/solution.py
@@ -46,7 +46,7 @@
     w_ref, master_ref, first_ref, second_ref, nm_ref, nf_ref, nsec_ref, actz,
     act_all, cot_all, cotp, actq, actg, cotg, cols, qcols, z_scr, conv_s, conv_r, spread_s, spread_r,
     gq, gacc, pub, slot_scr,
-    s_act, r_act, s_cot, r_cot, s_aq, r_aq, s_cp, r_cp, s_cv, r_cv, s_sp, r_sp, s_g, r_g, s_pub, r_pub, s_fw, s_az, r_az, s_in, s_out,
+    s_act, r_act, s_cot, r_cot, s_aq, r_aq, s_cp, r_cp, s_cv, r_cv, s_sp, r_sp, s_g, r_g, s_pub, r_pub, s_fw, s_az, r_az, s_in, s_out, s_aqf,
 ):
     d = lax.axis_index("dp")
     s = lax.axis_index("strip")
@@ -142,15 +142,21 @@
     for row in range(ns):
         actq[:, row * wid : (row + 1) * wid] = actz[row]
 
+    half = dp // 2
+
     def aq_copy(j, block):
-        return copy(actq, actg.at[block], s_aq.at[j], r_aq.at[block], (j, s))
+        return copy(actg.at[block], actg.at[block], s_aq.at[j], r_aq.at[block], (j, s))
+
+    def aqf_copy(block):
+        return copy(actg.at[block], actg.at[block], s_aqf.at[block], r_aq.at[block], (sibling, s))
 
     def send_aq(i, c):
-        aq_copy(dp_peer(i), d).start()
-        return c
-
-    lax.fori_loop(1, dp, send_aq, 0)
+        aq_copy(dp_peer(2 * i), d).start()
+        return c
+
     actg[d] = actq[...]
+    lax.fori_loop(1, half, send_aq, 0)
+    aqf_copy(d).start()
 
     for i in range(1, ns):
         act_copy(i, s).start()
@@ -183,20 +189,29 @@
     def grad_of(j):
         fill_cols(actg[j].astype(f32), qcols, wid)
         gacc[...] += lax.dot_general(
-            cotg[j], qcols[...], (((1,), (1,)), ((), ())), preferred_element_type=f32
+            qcols[...], cotg[j], (((1,), (1,)), ((), ())), preferred_element_type=f32
         )
 
     grad_of(d)
 
-    def grad_step(i, c):
-        j = dp_peer(i)
+    def grad_near(i, c):
+        j = dp_peer(2 * i)
+        aq_copy(j, j).wait_recv()
+        aqf_copy(j).start()
         cp_copy(j, j).wait_recv()
-        aq_copy(j, j).wait_recv()
         grad_of(j)
         return c
 
-    lax.fori_loop(1, dp, grad_step, 0)
-    gq[s] = (gacc[...] * (1.0 / math.sqrt(dp * ns * wid))).astype(bf16)
+    def grad_far(i, c):
+        j = lax.rem(sibling + 2 * i, dp)
+        aqf_copy(j).wait_recv()
+        cp_copy(j, j).wait_recv()
+        grad_of(j)
+        return c
+
+    lax.fori_loop(1, half, grad_near, 0)
+    lax.fori_loop(0, half, grad_far, 0)
+    gq[s] = (gacc[...].T * (1.0 / math.sqrt(dp * ns * wid))).astype(bf16)
 
     def g_copy(i, block):
         return copy(gq.at[block], gq.at[block], s_g.at[i], r_g.at[block], (d, strip_peer(i)))
@@ -246,8 +261,6 @@
     def fw_copy(block):
         return copy(pub.at[block], pub.at[block], s_fw.at[block], r_pub.at[block], (sibling, s))
 
-    half = dp // 2
-
     def send_pub(i, c):
         pub_copy(i, dp_peer(2 * i), d).start()
         return c
@@ -311,7 +324,6 @@
     def left(i, c):
         j = dp_peer(i)
         cp_copy(j, d).wait_send()
-        aq_copy(j, d).wait_send()
         return c
 
     lax.fori_loop(1, dp, left, 0)
@@ -319,18 +331,25 @@
     def left_pub(i, c):
         pub_copy(i, dp_peer(2 * i), d).wait_send()
         fw_copy(dp_peer(2 * i)).wait_send()
+        aq_copy(dp_peer(2 * i), d).wait_send()
+        aqf_copy(dp_peer(2 * i)).wait_send()
         return c
 
     lax.fori_loop(1, half, left_pub, 0)
     fw_copy(d).wait_send()
+    aqf_copy(d).wait_send()
 
 
 def hand_over(*refs):
-    sems = refs[12]
-    copies = [pltpu.make_async_copy(refs[k], refs[6 + k], sems.at[k]) for k in range(6)]
-    for c in copies:
+    ins, outs, bufs, sem_in, sem_out = refs[:6], refs[6:12], refs[12:18], refs[18], refs[19]
+    reads = [pltpu.make_async_copy(ins[k], bufs[k], sem_in.at[k]) for k in range(6)]
+    writes = [pltpu.make_async_copy(bufs[k], outs[k], sem_out.at[k]) for k in range(6)]
+    for c in reads:
         c.start()
-    for c in copies:
+    for k in range(6):
+        reads[k].wait()
+        writes[k].start()
+    for c in writes:
         c.wait()
 
 
@@ -362,10 +381,10 @@
         pltpu.VMEM((ns, chans, wid), bf16),
         pltpu.VMEM((ns, chans, wid), bf16),
         pltpu.VMEM((ns, capp, 9 * part), bf16),
-        pltpu.VMEM((capp, 9 * part), f32),
+        pltpu.VMEM((9 * part, capp), f32),
         pltpu.VMEM((dp, capp, width), bf16),
         pltpu.VMEM((chans, 1), jnp.int32),
-    ] + [dma(n) for n in (ns, ns, ns, ns, dp, dp, dp, dp, ns, ns, ns, ns, ns, ns, dp, dp, dp, ns, ns, 4, 3)]
+    ] + [dma(n) for n in (ns, ns, ns, ns, dp, dp, dp, dp, ns, ns, ns, ns, ns, ns, dp, dp, dp, ns, ns, 4, 3, dp)]
     made = pl.pallas_call(
             functools.partial(kernel, dp, ns, cap, capp),
             out_shape=[
@@ -385,7 +404,7 @@
         out_shape=[jax.ShapeDtypeStruct(a.shape, a.dtype) for a in arrays],
         in_specs=[anywhere] * 6,
         out_specs=[anywhere] * 6,
-        scratch_shapes=[pltpu.SemaphoreType.DMA((6,))],
+        scratch_shapes=[pltpu.VMEM(a.shape, a.dtype) for a in arrays] + [dma(6), dma(6)],
     )(*made)
     return tuple(results)
 

time: 129 us -> 55.6 us (0.43)
  the two profiles are of different devices: /device:TPU:0 before, /device:TPU:29 now
where the time goes in v3:
time: 55.6 us; the launch traced here: 55.4 us
  Pallas kernels  54.8 us (99%)
  between operations  0.64 us (1%)
    pallas_call x1, Pallas kernels, local(): pl.pallas_call(functools.partial(kernel, dp, ns, cap, capp), out_shape=[j...  52.2 us
    pallas_call x1, Pallas kernels, local(): pl.pallas_call(hand_over, out_shape=[jax.ShapeDtypeStruct(a.shape, a.dtyp...  2.57 us

profile of v3, /device:TPU:29, one launch (start us, length us, event | category | flops | bytes accessed | tf_op | source)
XLA Modules:
  0.0 55.4 jit_solution(3031798500929605694)
XLA Ops:
  0.6 52.2 %shard_map.118 = (bf16[1,1,320,128]{3,2,1,0:T(8,128)(2,1)}, bf16[1,1,320,128]{3,2,1,0:T(8,128)(2,1)}, bf16[80,2880]{1,0:T(8,128)(2,1)}, f32[42,2880]{1,0:T(8,128...) custom-call(bf16[1,1,320,128]{3,2,1,0:T(8,128)(2,1)} %lat_ref.1, bf16[1,1,320,128]{3,2,1,0:T(8,128)(2,1)} %cot_ref.1, ...), custom_call_target="tpu_custom_call" | custom-call | flops 1000000000 | bytes 6000000 | tf_op jit(solution)/shard_map/pallas_call | solution.py:388
  52.8 2.6 %shard_map.119 = (bf16[1,1,320,128]{3,2,1,0:T(8,128)(2,1)}, bf16[1,1,320,128]{3,2,1,0:T(8,128)(2,1)}, bf16[80,2880]{1,0:T(8,128)(2,1)}, f32[42,2880]{1,0:T(8,128...) custom-call(bf16[1,1,320,128]{3,2,1,0:T(8,128)(2,1)} %get-tuple-element.12.refs_0_, ...), custom_call_target="tpu_custom_call" | custom-call | tf_op jit(solution)/shard_map/pallas_call | solution.py:402

commit v4 on v3

--- a/solution.py
+++ b/solution.py
@@ -45,7 +45,7 @@
     out_ref, gin_ref, nw_ref, nm_hbm, nf_hbm, nsec_hbm,
     w_ref, master_ref, first_ref, second_ref, nm_ref, nf_ref, nsec_ref, actz,
     act_all, cot_all, cotp, actq, actg, cotg, cols, qcols, z_scr, conv_s, conv_r, spread_s, spread_r,
-    gq, gacc, pub, slot_scr,
+    gq, gacc, pub, slot_scr, wacc,
     s_act, r_act, s_cot, r_cot, s_aq, r_aq, s_cp, r_cp, s_cv, r_cv, s_sp, r_sp, s_g, r_g, s_pub, r_pub, s_fw, s_az, r_az, s_in, s_out, s_aqf,
 ):
     d = lax.axis_index("dp")
@@ -213,11 +213,15 @@
     lax.fori_loop(0, half, grad_far, 0)
     gq[s] = (gacc[...].T * (1.0 / math.sqrt(dp * ns * wid))).astype(bf16)
 
-    def g_copy(i, block):
-        return copy(gq.at[block], gq.at[block], s_g.at[i], r_g.at[block], (d, strip_peer(i)))
-
-    for i in range(1, ns):
-        g_copy(i, s).start()
+    chunks = capp // 16
+
+    def g_copy(i, block, c):
+        src = gq.at[block, 16 * c : 16 * c + 16, :]
+        return copy(src, src, s_g.at[c * ns + i], r_g.at[c * ns + block], (d, strip_peer(i)))
+
+    for c in range(chunks):
+        for i in range(1, ns):
+            g_copy(i, s, c).start()
     for i in range(1, ns):
         act_copy(i, strip_peer(i)).wait_recv()
     whole = jnp.concatenate([act_all[row] for row in range(ns)], axis=1).astype(f32)
@@ -229,50 +233,84 @@
     def cv_copy(i, block):
         return copy(conv_s.at[strip_peer(i)], conv_r.at[block], s_cv.at[i], r_cv.at[block], (d, strip_peer(i)))
 
-    for i in range(1, ns):
-        g_copy(i, strip_peer(i)).wait_recv()
+    for load in loads[1:]:
+        load.wait()
+
+    def pub_copy(i, j, block, c):
+        src = pub.at[block, 16 * c : 16 * c + 16, :]
+        return copy(src, src, s_pub.at[c * dp + i], r_pub.at[c * dp + block], (j, s))
+
+    def fw_copy(block, c):
+        src = pub.at[block, 16 * c : 16 * c + 16, :]
+        return copy(src, src, s_fw.at[c * dp + block], r_pub.at[c * dp + block], (sibling, s))
+
+    for c in range(chunks):
+        low, high = 16 * c, min(16 * c + 16, cap)
+        for i in range(1, ns):
+            g_copy(i, strip_peer(i), c).wait_recv()
+        pieces = []
+        for tap in range(9):
+            for row in range(ns):
+                pieces.append(gq[row, low : low + 16, tap * part : (tap + 1) * part])
+        grads = jnp.concatenate(pieces, axis=1).astype(f32)[: high - low]
+        kept = keep[low:high]
+        first = first_ref[low:high, :]
+        second = second_ref[low:high, :]
+        master = master_ref[low:high, :]
+        first_new = beta_first * first + (1.0 - beta_first) * grads
+        second_new = beta_second * second + (1.0 - beta_second) * grads * grads
+        update = learn_rate * (first_new / bias_first) / (jnp.sqrt(second_new / bias_second) + epsilon)
+        master_new = jnp.where(kept, master - update, master)
+        full = master_new
+        if high - low < 16:
+            full = jnp.concatenate(
+                [master_new, jnp.zeros((16 - high + low, master_new.shape[1]), f32)], axis=0
+            )
+        pub[d, low : low + 16, :] = full.astype(bf16)
+
+        def send_pub(i, carry, c=c):
+            pub_copy(i, dp_peer(2 * i), d, c).start()
+            return carry
+
+        lax.fori_loop(1, half, send_pub, 0)
+        fw_copy(d, c).start()
+        nm_ref[low:high, :] = master_new
+        nf_ref[low:high, :] = jnp.where(kept, first_new, first)
+        nsec_ref[low:high, :] = jnp.where(kept, second_new, second)
     for i in range(1, ns):
         cv_copy(i, s).start()
         sp_copy(i, s).start()
-    for load in loads[1:]:
-        load.wait()
-    pieces = []
-    for tap in range(9):
-        for row in range(ns):
-            pieces.append(gq[row, :, tap * part : (tap + 1) * part])
-    grads = jnp.concatenate(pieces, axis=1).astype(f32)[:cap]
-    first = first_ref[...]
-    second = second_ref[...]
-    master = master_ref[...]
-    first_new = beta_first * first + (1.0 - beta_first) * grads
-    second_new = beta_second * second + (1.0 - beta_second) * grads * grads
-    update = learn_rate * (first_new / bias_first) / (jnp.sqrt(second_new / bias_second) + epsilon)
-    master_new = jnp.where(keep, master - update, master)
-    nm_ref[...] = master_new
-    nf_ref[...] = jnp.where(keep, first_new, first)
-    nsec_ref[...] = jnp.where(keep, second_new, second)
-    pub[d] = jnp.concatenate(
-        [master_new, jnp.zeros((capp - cap, master_new.shape[1]), f32)], axis=0
-    ).astype(bf16)
-
-    def pub_copy(i, j, block):
-        return copy(pub.at[block], pub.at[block], s_pub.at[i], r_pub.at[block], (j, s))
-
-    def fw_copy(block):
-        return copy(pub.at[block], pub.at[block], s_fw.at[block], r_pub.at[block], (sibling, s))
-
-    def send_pub(i, c):
-        pub_copy(i, dp_peer(2 * i), d).start()
-        return c
-
-    lax.fori_loop(1, half, send_pub, 0)
-    fw_copy(d).start()
     stores = [
         pltpu.make_async_copy(src, dst, s_out.at[k])
         for k, (src, dst) in enumerate(((nm_ref, nm_hbm), (nf_ref, nf_hbm), (nsec_ref, nsec_hbm)))
     ]
     for store in stores:
         store.start()
+
+    slots = slot_scr[mine, :]
+
+    def wanted(j):
+        want = jnp.where(
+            lax.broadcasted_iota(jnp.int32, (part, capp), 1) + j * capp == slots, 1.0, 0.0
+        ).astype(bf16)
+        return jnp.dot(want, pub[j], preferred_element_type=f32)
+
+    wacc[...] = wanted(d)
+    for c in range(chunks):
+
+        def forward(i, carry, c=c):
+            j = dp_peer(2 * i)
+            pub_copy(i, j, j, c).wait_recv()
+            fw_copy(j, c).start()
+            return carry
+
+        lax.fori_loop(1, half, forward, 0)
+
+    def near(i, carry):
+        wacc[...] += wanted(dp_peer(2 * i))
+        return carry
+
+    lax.fori_loop(1, half, near, 0)
 
     for i in range(1, ns):
         cv_copy(i, strip_peer(i)).wait_recv()
@@ -289,27 +327,15 @@
         cot_ref[0, 0].astype(f32) + back * (sig * (1.0 + pix * (1.0 - sig)))
     ).astype(bf16)
 
-    def forward(i, c):
-        j = dp_peer(2 * i)
-        pub_copy(i, j, j).wait_recv()
-        fw_copy(j).start()
-        return c
-
-    lax.fori_loop(1, half, forward, 0)
-    base = sibling
-
-    def arrive(i, c):
-        fw_copy(lax.rem(base + 2 * i, dp)).wait_recv()
-        return c
-
-    lax.fori_loop(0, half, arrive, 0)
-    slots = slot_scr[mine, :]
-    want = jnp.where(
-        lax.broadcasted_iota(jnp.int32, (part, dp * capp), 1) == slots, 1.0, 0.0
-    ).astype(bf16)
-    nw_ref[...] = jnp.dot(
-        want, pub[...].reshape(dp * capp, pub.shape[2]), preferred_element_type=f32
-    ).astype(bf16)
+    def far(i, carry):
+        j = lax.rem(sibling + 2 * i, dp)
+        for c in range(chunks):
+            fw_copy(j, c).wait_recv()
+        wacc[...] += wanted(j)
+        return carry
+
+    lax.fori_loop(0, half, far, 0)
+    nw_ref[...] = wacc[...].astype(bf16)
 
     for store in stores:
         store.wait()
@@ -319,7 +345,8 @@
         cot_copy(i, s).wait_send()
         cv_copy(i, s).wait_send()
         sp_copy(i, s).wait_send()
-        g_copy(i, s).wait_send()
+        for c in range(chunks):
+            g_copy(i, s, c).wait_send()
 
     def left(i, c):
         j = dp_peer(i)
@@ -329,14 +356,16 @@
     lax.fori_loop(1, dp, left, 0)
 
     def left_pub(i, c):
-        pub_copy(i, dp_peer(2 * i), d).wait_send()
-        fw_copy(dp_peer(2 * i)).wait_send()
+        for k in range(chunks):
+            pub_copy(i, dp_peer(2 * i), d, k).wait_send()
+            fw_copy(dp_peer(2 * i), k).wait_send()
         aq_copy(dp_peer(2 * i), d).wait_send()
         aqf_copy(dp_peer(2 * i)).wait_send()
         return c
 
     lax.fori_loop(1, half, left_pub, 0)
-    fw_copy(d).wait_send()
+    for c in range(chunks):
+        fw_copy(d, c).wait_send()
     aqf_copy(d).wait_send()
 
 
@@ -358,6 +387,7 @@
     cap = master.shape[0]
     capp = -(-cap // 16) * 16
     part = chans // ns
+    chunks = capp // 16
     width = weight.shape[1]
     pixels = ns * wid
     dma = lambda n: pltpu.SemaphoreType.DMA((n,))
@@ -384,7 +414,10 @@
         pltpu.VMEM((9 * part, capp), f32),
         pltpu.VMEM((dp, capp, width), bf16),
         pltpu.VMEM((chans, 1), jnp.int32),
-    ] + [dma(n) for n in (ns, ns, ns, ns, dp, dp, dp, dp, ns, ns, ns, ns, ns, ns, dp, dp, dp, ns, ns, 4, 3, dp)]
+        pltpu.VMEM((part, width), f32),
+    ] + [dma(n) for n in (
+        ns, ns, ns, ns, dp, dp, dp, dp, ns, ns, ns, ns, ns * chunks, ns * chunks,
+        dp * chunks, dp * chunks, dp * chunks, ns, ns, 4, 3, dp)]
     made = pl.pallas_call(
             functools.partial(kernel, dp, ns, cap, capp),
             out_shape=[

time: 55.6 us -> 53.4 us (0.960)
  the two profiles are of different devices: /device:TPU:29 before, /device:TPU:0 now
where the time goes in v4:
time: 53.4 us; the launch traced here: 53.2 us
  Pallas kernels  52.5 us (98%)
  between operations  0.64 us (1%)
    pallas_call x1, Pallas kernels, local(): pl.pallas_call(functools.partial(kernel, dp, ns, cap, capp), out_shape=[j...  50 us
    pallas_call x1, Pallas kernels, local(): pl.pallas_call(hand_over, out_shape=[jax.ShapeDtypeStruct(a.shape, a.dtyp...  2.57 us

profile of v4, /device:TPU:0, one launch (start us, length us, event | category | flops | bytes accessed | tf_op | source)
XLA Modules:
  0.0 53.2 jit_solution(4961596581193026368)
XLA Ops:
  0.6 50.0 %shard_map.118 = (bf16[1,1,320,128]{3,2,1,0:T(8,128)(2,1)}, bf16[1,1,320,128]{3,2,1,0:T(8,128)(2,1)}, bf16[80,2880]{1,0:T(8,128)(2,1)}, f32[42,2880]{1,0:T(8,128...) custom-call(bf16[1,1,320,128]{3,2,1,0:T(8,128)(2,1)} %lat_ref.1, bf16[1,1,320,128]{3,2,1,0:T(8,128)(2,1)} %cot_ref.1, ...), custom_call_target="tpu_custom_call" | custom-call | flops 1000000000 | bytes 6000000 | tf_op jit(solution)/shard_map/pallas_call | solution.py:421
  50.6 2.6 %shard_map.119 = (bf16[1,1,320,128]{3,2,1,0:T(8,128)(2,1)}, bf16[1,1,320,128]{3,2,1,0:T(8,128)(2,1)}, bf16[80,2880]{1,0:T(8,128)(2,1)}, f32[42,2880]{1,0:T(8,128...) custom-call(bf16[1,1,320,128]{3,2,1,0:T(8,128)(2,1)} %get-tuple-element.12.refs_0_, ...), custom_call_target="tpu_custom_call" | custom-call | tf_op jit(solution)/shard_map/pallas_call | solution.py:435

commit v5 on v4

--- a/solution.py
+++ b/solution.py
@@ -44,7 +44,7 @@
     lat_ref, cot_ref, w_hbm, master_hbm, first_hbm, second_hbm, own_ref,
     out_ref, gin_ref, nw_ref, nm_hbm, nf_hbm, nsec_hbm,
     w_ref, master_ref, first_ref, second_ref, nm_ref, nf_ref, nsec_ref, actz,
-    act_all, cot_all, cotp, actq, actg, cotg, cols, qcols, z_scr, conv_s, conv_r, spread_s, spread_r,
+    act_all, cot_all, cotp, actg, cotg, cols, qcols, z_scr, conv_s, conv_r, spread_s, spread_r,
     gq, gacc, pub, slot_scr, wacc,
     s_act, r_act, s_cot, r_cot, s_aq, r_aq, s_cp, r_cp, s_cv, r_cv, s_sp, r_sp, s_g, r_g, s_pub, r_pub, s_fw, s_az, r_az, s_in, s_out, s_aqf,
 ):
@@ -97,14 +97,13 @@
     def cot_copy(i, block):
         return copy(cot_all.at[block], cot_all.at[block], s_cot.at[i], r_cot.at[block], (d, strip_peer(i)))
 
-    for i in range(1, ns):
-        cot_copy(i, s).start()
     def az_copy(i, block):
         rows = pl.ds(pl.multiple_of(strip_peer(i) * part, part), part)
         return copy(act_all.at[s, rows, :], actz.at[block], s_az.at[i], r_az.at[block], (d, strip_peer(i)))
 
     for i in range(1, ns):
         az_copy(i, s).start()
+        cot_copy(i, s).start()
 
     orow = own_ref[...].reshape(1, chans)
     a0 = lax.broadcasted_iota(jnp.int32, (chans, chans), 0)
@@ -121,42 +120,45 @@
         lax.broadcasted_iota(jnp.int32, (dp * capp, chans), 0) == slot_row, 1.0, 0.0
     ).astype(bf16)
 
-    for i in range(1, ns):
-        cot_copy(i, strip_peer(i)).wait_recv()
-    for row in range(ns):
+    half = dp // 2
+
+    def cp_copy(j, block, row):
+        return copy(
+            cotp.at[row, j], cotg.at[block, row], s_cp.at[row * dp + j], r_cp.at[row * dp + block], (j, s)
+        )
+
+    def aq_copy(j, block, row):
+        src = actg.at[block, row]
+        return copy(src, src, s_aq.at[row * dp + j], r_aq.at[row * dp + block], (j, s))
+
+    def aqf_copy(block, row):
+        src = actg.at[block, row]
+        at = row * dp + block
+        return copy(src, src, s_aqf.at[at], r_aq.at[at], (sibling, s))
+
+    for near_by in range(ns):
+        row = strip_peer(near_by)
+        if near_by:
+            az_copy(near_by, row).wait_recv()
+        actg[d, row] = actz[row]
+
+        def send_aq(i, c, row=row):
+            aq_copy(dp_peer(2 * i), d, row).start()
+            return c
+
+        lax.fori_loop(1, half, send_aq, 0)
+        aqf_copy(d, row).start()
+        if near_by:
+            cot_copy(near_by, row).wait_recv()
         chosen = jnp.dot(pick, cot_all[row], preferred_element_type=f32).astype(bf16)
-        cotp[:, :, row * wid : (row + 1) * wid] = chosen.reshape(dp, capp, wid)
-
-    def cp_copy(j, block):
-        return copy(cotp.at[j], cotg.at[block], s_cp.at[j], r_cp.at[block], (j, s))
-
-    def send_cp(i, c):
-        cp_copy(dp_peer(i), d).start()
-        return c
-
-    lax.fori_loop(1, dp, send_cp, 0)
-    cotg[d] = cotp[d]
-
-    for i in range(1, ns):
-        az_copy(i, strip_peer(i)).wait_recv()
-    for row in range(ns):
-        actq[:, row * wid : (row + 1) * wid] = actz[row]
-
-    half = dp // 2
-
-    def aq_copy(j, block):
-        return copy(actg.at[block], actg.at[block], s_aq.at[j], r_aq.at[block], (j, s))
-
-    def aqf_copy(block):
-        return copy(actg.at[block], actg.at[block], s_aqf.at[block], r_aq.at[block], (sibling, s))
-
-    def send_aq(i, c):
-        aq_copy(dp_peer(2 * i), d).start()
-        return c
-
-    actg[d] = actq[...]
-    lax.fori_loop(1, half, send_aq, 0)
-    aqf_copy(d).start()
+        cotp[row] = chosen.reshape(dp, capp, wid)
+
+        def send_cp(i, c, row=row):
+            cp_copy(dp_peer(i), d, row).start()
+            return c
+
+        lax.fori_loop(1, dp, send_cp, 0)
+        cotg[d, row] = cotp[row, d]
 
     for i in range(1, ns):
         act_copy(i, s).start()
@@ -187,25 +189,29 @@
     gacc[...] = jnp.zeros_like(gacc)
 
     def grad_of(j):
-        fill_cols(actg[j].astype(f32), qcols, wid)
+        fill_cols(jnp.concatenate([actg[j, row] for row in range(ns)], axis=1).astype(f32), qcols, wid)
+        rows = jnp.concatenate([cotg[j, row] for row in range(ns)], axis=1)
         gacc[...] += lax.dot_general(
-            qcols[...], cotg[j], (((1,), (1,)), ((), ())), preferred_element_type=f32
+            qcols[...], rows, (((1,), (1,)), ((), ())), preferred_element_type=f32
         )
 
     grad_of(d)
 
     def grad_near(i, c):
         j = dp_peer(2 * i)
-        aq_copy(j, j).wait_recv()
-        aqf_copy(j).start()
-        cp_copy(j, j).wait_recv()
+        for row in range(ns):
+            aq_copy(j, j, row).wait_recv()
+            aqf_copy(j, row).start()
+        for row in range(ns):
+            cp_copy(j, j, row).wait_recv()
         grad_of(j)
         return c
 
     def grad_far(i, c):
         j = lax.rem(sibling + 2 * i, dp)
-        aqf_copy(j).wait_recv()
-        cp_copy(j, j).wait_recv()
+        for row in range(ns):
+            aqf_copy(j, row).wait_recv()
+            cp_copy(j, j, row).wait_recv()
         grad_of(j)
         return c
 
@@ -350,7 +356,8 @@
 
     def left(i, c):
         j = dp_peer(i)
-        cp_copy(j, d).wait_send()
+        for row in range(ns):
+            cp_copy(j, d, row).wait_send()
         return c
 
     lax.fori_loop(1, dp, left, 0)
@@ -359,14 +366,16 @@
         for k in range(chunks):
             pub_copy(i, dp_peer(2 * i), d, k).wait_send()
             fw_copy(dp_peer(2 * i), k).wait_send()
-        aq_copy(dp_peer(2 * i), d).wait_send()
-        aqf_copy(dp_peer(2 * i)).wait_send()
+        for row in range(ns):
+            aq_copy(dp_peer(2 * i), d, row).wait_send()
+            aqf_copy(dp_peer(2 * i), row).wait_send()
         return c
 
     lax.fori_loop(1, half, left_pub, 0)
     for c in range(chunks):
         fw_copy(d, c).wait_send()
-    aqf_copy(d).wait_send()
+    for row in range(ns):
+        aqf_copy(d, row).wait_send()
 
 
 def hand_over(*refs):
@@ -399,10 +408,9 @@
         pltpu.VMEM((ns, part, wid), bf16),
         pltpu.VMEM((ns, chans, wid), bf16),
         pltpu.VMEM((ns, chans, wid), bf16),
-        pltpu.VMEM((dp, capp, pixels), bf16),
-        pltpu.VMEM((part, pixels), bf16),
-        pltpu.VMEM((dp, part, pixels), bf16),
-        pltpu.VMEM((dp, capp, pixels), bf16),
+        pltpu.VMEM((ns, dp, capp, wid), bf16),
+        pltpu.VMEM((dp, ns, part, wid), bf16),
+        pltpu.VMEM((dp, ns, capp, wid), bf16),
         pltpu.VMEM((9 * chans, pixels), bf16),
         pltpu.VMEM((9 * part, pixels), bf16),
         pltpu.VMEM((9 * chans, pixels), f32),
@@ -416,8 +424,8 @@
         pltpu.VMEM((chans, 1), jnp.int32),
         pltpu.VMEM((part, width), f32),
     ] + [dma(n) for n in (
-        ns, ns, ns, ns, dp, dp, dp, dp, ns, ns, ns, ns, ns * chunks, ns * chunks,
-        dp * chunks, dp * chunks, dp * chunks, ns, ns, 4, 3, dp)]
+        ns, ns, ns, ns, ns * dp, ns * dp, ns * dp, ns * dp, ns, ns, ns, ns, ns * chunks, ns * chunks,
+        dp * chunks, dp * chunks, dp * chunks, ns, ns, 4, 3, ns * dp)]
     made = pl.pallas_call(
             functools.partial(kernel, dp, ns, cap, capp),
             out_shape=[

time: 53.4 us -> 52.4 us (0.981)
  Pallas kernels: 52.5 us -> 51.5 us
    pallas_call x1, Pallas kernels: 50 us -> 49 us  [local(): pl.pallas_call(functools.partial(kernel, dp, ns, cap, capp), out_shape=[j...]
where the time goes in v5:
time: 52.4 us; the launch traced here: 52.2 us
  Pallas kernels  51.5 us (98%)
  between operations  0.64 us (1%)
    pallas_call x1, Pallas kernels, local(): pl.pallas_call(functools.partial(kernel, dp, ns, cap, capp), out_shape=[j...  49 us
    pallas_call x1, Pallas kernels, local(): pl.pallas_call(hand_over, out_shape=[jax.ShapeDtypeStruct(a.shape, a.dtyp...  2.57 us

profile of v5, /device:TPU:0, one launch (start us, length us, event | category | flops | bytes accessed | tf_op | source)
XLA Modules:
  0.0 52.2 jit_solution(5855241997789024409)
XLA Ops:
  0.6 49.0 %shard_map.118 = (bf16[1,1,320,128]{3,2,1,0:T(8,128)(2,1)}, bf16[1,1,320,128]{3,2,1,0:T(8,128)(2,1)}, bf16[80,2880]{1,0:T(8,128)(2,1)}, f32[42,2880]{1,0:T(8,128...) custom-call(bf16[1,1,320,128]{3,2,1,0:T(8,128)(2,1)} %lat_ref.1, bf16[1,1,320,128]{3,2,1,0:T(8,128)(2,1)} %cot_ref.1, ...), custom_call_target="tpu_custom_call" | custom-call | flops 1000000000 | bytes 6000000 | tf_op jit(solution)/shard_map/pallas_call | solution.py:429
  49.6 2.6 %shard_map.119 = (bf16[1,1,320,128]{3,2,1,0:T(8,128)(2,1)}, bf16[1,1,320,128]{3,2,1,0:T(8,128)(2,1)}, bf16[80,2880]{1,0:T(8,128)(2,1)}, f32[42,2880]{1,0:T(8,128...) custom-call(bf16[1,1,320,128]{3,2,1,0:T(8,128)(2,1)} %get-tuple-element.12.refs_0_, ...), custom_call_target="tpu_custom_call" | custom-call | tf_op jit(solution)/shard_map/pallas_call | solution.py:443

commit v6 on v5

--- a/solution.py
+++ b/solution.py
@@ -228,17 +228,6 @@
     for c in range(chunks):
         for i in range(1, ns):
             g_copy(i, s, c).start()
-    for i in range(1, ns):
-        act_copy(i, strip_peer(i)).wait_recv()
-    whole = jnp.concatenate([act_all[row] for row in range(ns)], axis=1).astype(f32)
-    fill_cols(whole, cols, wid)
-    conv = jnp.dot(w_ref[...], cols[...], preferred_element_type=f32)
-    for row in range(ns):
-        conv_s[row] = conv[:, row * wid : (row + 1) * wid].astype(bf16)
-
-    def cv_copy(i, block):
-        return copy(conv_s.at[strip_peer(i)], conv_r.at[block], s_cv.at[i], r_cv.at[block], (d, strip_peer(i)))
-
     for load in loads[1:]:
         load.wait()
 
@@ -284,8 +273,20 @@
         nf_ref[low:high, :] = jnp.where(kept, first_new, first)
         nsec_ref[low:high, :] = jnp.where(kept, second_new, second)
     for i in range(1, ns):
+        sp_copy(i, s).start()
+    for i in range(1, ns):
+        act_copy(i, strip_peer(i)).wait_recv()
+    whole = jnp.concatenate([act_all[row] for row in range(ns)], axis=1).astype(f32)
+    fill_cols(whole, cols, wid)
+    conv = jnp.dot(w_ref[...], cols[...], preferred_element_type=f32)
+    for row in range(ns):
+        conv_s[row] = conv[:, row * wid : (row + 1) * wid].astype(bf16)
+
+    def cv_copy(i, block):
+        return copy(conv_s.at[strip_peer(i)], conv_r.at[block], s_cv.at[i], r_cv.at[block], (d, strip_peer(i)))
+
+    for i in range(1, ns):
         cv_copy(i, s).start()
-        sp_copy(i, s).start()
     stores = [
         pltpu.make_async_copy(src, dst, s_out.at[k])
         for k, (src, dst) in enumerate(((nm_ref, nm_hbm), (nf_ref, nf_hbm), (nsec_ref, nsec_hbm)))

time: 52.4 us -> 52.3 us (level)
  no operation moved by 1% of the time
where the time goes in v6:
time: 52.3 us; the launch traced here: 52.2 us
  Pallas kernels  51.5 us (98%)
  between operations  0.64 us (1%)
    pallas_call x1, Pallas kernels, local(): pl.pallas_call(functools.partial(kernel, dp, ns, cap, capp), out_shape=[j...  48.9 us
    pallas_call x1, Pallas kernels, local(): pl.pallas_call(hand_over, out_shape=[jax.ShapeDtypeStruct(a.shape, a.dtyp...  2.57 us

profile of v6, /device:TPU:0, one launch (start us, length us, event | category | flops | bytes accessed | tf_op | source)
XLA Modules:
  0.0 52.2 jit_solution(1783448125127156146)
XLA Ops:
  0.6 48.9 %shard_map.118 = (bf16[1,1,320,128]{3,2,1,0:T(8,128)(2,1)}, bf16[1,1,320,128]{3,2,1,0:T(8,128)(2,1)}, bf16[80,2880]{1,0:T(8,128)(2,1)}, f32[42,2880]{1,0:T(8,128...) custom-call(bf16[1,1,320,128]{3,2,1,0:T(8,128)(2,1)} %lat_ref.1, bf16[1,1,320,128]{3,2,1,0:T(8,128)(2,1)} %cot_ref.1, ...), custom_call_target="tpu_custom_call" | custom-call | flops 1000000000 | bytes 6000000 | tf_op jit(solution)/shard_map/pallas_call | solution.py:430
  49.6 2.6 %shard_map.119 = (bf16[1,1,320,128]{3,2,1,0:T(8,128)(2,1)}, bf16[1,1,320,128]{3,2,1,0:T(8,128)(2,1)}, bf16[80,2880]{1,0:T(8,128)(2,1)}, f32[42,2880]{1,0:T(8,128...) custom-call(bf16[1,1,320,128]{3,2,1,0:T(8,128)(2,1)} %get-tuple-element.12.refs_0_, ...), custom_call_target="tpu_custom_call" | custom-call | tf_op jit(solution)/shard_map/pallas_call | solution.py:444
